TPU v7x, 128 devices: a whole 4x4x4 slice. The times are simulated.
128 devices in a mesh: dp: 4 (over y_hi, core), fsdp: 32 (over x, z, y_lo).
Axes of the slice: x: 4, y: 4 (y_hi: 2, y_lo: 2; y = y_hi * 2 + y_lo), z: 4, core: 2. Of those that a mesh axis runs over, the one named last changes fastest.
Arguments:
- normed: bfloat16 [131072, 4096], P(('dp', 'fsdp')), may hold values from -24 to 24
- k_weight: bfloat16 [4096, 512], P('fsdp'), may hold values from -0.09375 to 0.09375
- k_gain: float32 [128], replicated, may hold values from 0.5 to 1.5
- probe_k: bfloat16 [4096, 512], P('fsdp'), may hold values from -6 to 6
- probe_v: bfloat16 [4096, 512], P('fsdp'), may hold values from -6 to 6
Outputs:
- diag_k: float32 [4096, 512], P(('dp', 'fsdp'))
- diag_v: float32 [4096, 512], P(('dp', 'fsdp'))
All inputs are finite; a program needn't handle non-finite values.
Results may differ from a plain program's by a relative error of at most 0.00075.
Values may be sent and summed in bfloat16 or wider, within the bound.
A program may use at most 128 MiB of HBM per device.

v0:
```python
import jax
import jax.numpy as jnp
from jax import lax
from jax.sharding import PartitionSpec as P

HEAD = 128


EPS = 1e-06


def cotangent(raw, tangent_k, tangent_v, gain):
    rows = raw.shape[0]
    heads = raw.shape[1] // HEAD
    alpha = raw.reshape(rows, heads, HEAD)
    delta = tangent_k.reshape(rows, heads, HEAD)
    inv = lax.rsqrt(jnp.mean(alpha * alpha, axis=-1, keepdims=True) + EPS)
    cubed = inv * inv * inv
    key_tan = gain * (
        delta * inv - alpha * (jnp.sum(alpha * delta, axis=-1, keepdims=True) / HEAD) * cubed
    )
    back = (
        gain * key_tan * inv
        - alpha * (jnp.sum(alpha * gain * key_tan, axis=-1, keepdims=True) / HEAD) * cubed
    )
    return jnp.concatenate([back.reshape(rows, heads * HEAD), tangent_v], axis=1).astype(
        jnp.bfloat16
    )


def shards(normed, k_weight, k_gain, probe_k, probe_v):
    rows = normed.shape[0]
    width = k_weight.shape[1]
    groups = lax.axis_size("dp")
    members = lax.axis_size("fsdp")
    raw = jnp.dot(
        normed,
        lax.all_gather(k_weight, "fsdp", axis=0, tiled=True),
        preferred_element_type=jnp.float32,
    )
    full_k, full_v = (
        lax.all_gather(probe_k, "fsdp", axis=0, tiled=True),
        lax.all_gather(probe_v, "fsdp", axis=0, tiled=True),
    )
    probes = jnp.concatenate([full_k, full_v], axis=1)
    tangent = jnp.dot(normed, probes, preferred_element_type=jnp.float32)
    cot = cotangent(raw, tangent[:, :width], tangent[:, width:], k_gain)
    features = probes.shape[0]
    share = features // (groups * members)
    total_tokens = rows * groups * members
    term = lax.dot_general(
        normed, cot, (((0,), (0,)), ((), ())), preferred_element_type=jnp.float32
    )
    term = term * probes.astype(jnp.float32)
    blocks = term.reshape(groups, members, share, 2 * width)
    reduced = lax.psum_scatter(blocks, "fsdp", scatter_dimension=1, tiled=True)
    reduced = lax.psum_scatter(reduced, "dp", scatter_dimension=0, tiled=True)
    summed = reduced.reshape(share, 2 * width)
    estimate = summed / total_tokens
    return (estimate[:, :width], estimate[:, width:])


def solution(mesh):
    return jax.shard_map(
        shards,
        mesh=mesh,
        in_specs=(P(("dp", "fsdp"), None), P("fsdp", None), P(), P("fsdp", None), P("fsdp", None)),
        out_specs=(P(("dp", "fsdp"), None), P(("dp", "fsdp"), None)),
        check_vma=False,
    )
```

profile of v0, /device:TPU:1, one launch (start us, length us, event | category | flops | bytes accessed | tf_op | source)
XLA Modules:
  0.0 1286.1 jit_solution(9887786625580293198)
XLA Ops:
  7.2 0.0 all-gather.4.cloned.1.call-start
  7.2 1.6 copy.13
  8.9 0.0 all-gather.4.cloned.1.call-update
  8.9 0.0 all-gather.6.cloned.1.call-start
  8.9 1.6 copy.14
  10.6 0.0 all-gather.6.cloned.1.call-update
  10.6 0.0 all-gather.8.cloned.1.call-start
  10.7 0.7 all-gather.8.cloned.1.call-update
  11.3 0.0 all-reduce.3.cloned.1.call-start
  11.4 0.7 broadcast_bitcast_fusion
  12.1 131.0 %all-gather.4.cloned.1.call-done = bf16[4096,512]{0,1:T(8,128)(2,1)} async-done(((bf16[128,512]{0,1:T(8,128)(2,1)}), bf16[4096,512]{0,1:T(8,128)(2,1)}) %all-gather.4.cloned.1.call-update) | async-done | bytes 4194320 | tf_op jit(solution)/shard_map/all_gather | solution.py:42
  143.0 4.6 constant_dynamic-update-slice_fusion.1
  147.6 146.5 %all-gather.6.cloned.1.call-done = bf16[4096,512]{0,1:T(8,128)(2,1)} async-done(((bf16[128,512]{0,1:T(8,128)(2,1)}), bf16[4096,512]{0,1:T(8,128)(2,1)}) %all-gather.6.cloned.1.call-update) | async-done | bytes 4194320 | tf_op jit(solution)/shard_map/all_gather | solution.py:43
  294.1 4.7 constant_dynamic-update-slice_fusion
  298.8 12.6 convolution_bitcast_fusion
  311.4 0.0 copy-start
  311.4 2.0 copy-done
  313.4 0.2 slice.25
  313.6 0.0 copy-start.2
  313.6 138.5 %all-gather.8.cloned.1.call-done = bf16[4096,512]{1,0:T(8,128)(2,1)} async-done(((bf16[128,512]{1,0:T(8,128)(2,1)}), bf16[4096,512]{1,0:T(8,128)(2,1)}) %all-gather.8.cloned.1.call-update) | async-done | bytes 4194320 | tf_op jit(solution)/shard_map/all_gather | solution.py:38
  452.1 0.0 copy-start.1
  452.1 10.0 multiply_reduce_fusion.1
  462.2 0.0 copy-done.2
  462.2 0.0 copy-done.1
  462.2 0.7 multiply_reduce_fusion
  462.9 0.8 fusion.4
  463.7 17.5 %bitcast_multiply_fusion = f32[4096,1024]{0,1:T(8,128)} fusion(bf16[4096,1024]{0,1:T(8,128)(2,1)} %constant_dynamic-update-slice_fusion, bf16[1024,4096]{1,0:T(8,128)(2,1)} %param.5, bf16[1024,512]{0,1:T(8,128)(2,1)S(1)} %slice.25, bf16[1024,512]{0,1:T(8,128)(2,1)S(1)} %fusion.4), kind=kOutput, calls=%fused_computation | convolution fusion | flops 8602517504 | bytes 35651584 | tf_op jit(solution)/shard_map/dot_general | solution.py:51
  481.3 17.4 %copy.15 = f32[4096,1024]{1,0:T(8,128)} copy(f32[4096,1024]{0,1:T(8,128)} %bitcast_multiply_fusion) | data formatting | bytes 33554432 | tf_op jit(solution)/shard_map/mul | solution.py:54
  498.7 0.0 copy-start.3
  498.7 0.0 all-reduce.3.cloned.1.call-update
  498.7 0.0 reduce-scatter.5.cloned.1.call-start
  498.8 0.6 copy-done.3
  499.4 0.6 dynamic-slice
  499.9 744.7 %all-reduce.3.cloned.1.call-done = f32[4,32,32,1024]{3,2,1,0:T(8,128)} async-done(((f32[4,32,32,1024]{3,2,1,0:T(8,128)}), f32[4,32,32,1024]{3,2,1,0:T(8,128)}) %all-reduce.3.cloned.1.call-update) | async-done | bytes 16777232
  1244.6 2.5 constant_dynamic-slice_fusion
  1247.1 0.0 reduce-scatter.5.cloned.1.call-update
  1247.2 30.9 %reduce-scatter.5.cloned.1.call-done = f32[1,1,32,1024]{3,2,1,0:T(8,128)} async-done(((f32[4,1,32,1024]{3,2,1,0:T(8,128)}), f32[1,1,32,1024]{3,2,1,0:T(8,128)}) %reduce-scatter.5.cloned.1.call-update) | async-done | bytes 131088 | tf_op jit(solution)/shard_map/reduce_scatter | solution.py:57
  1278.0 0.9 multiply_bitcast_fusion
  1278.9 0.7 fusion.9
  (2 shorter events, 0.0 us)
Async XLA Ops:
  7.2 135.9 %all-gather.4.cloned.1.call-start = ((), (), s32[]{:S(2)}) async-start(), calls=%async_computation.1 | async-start | bytes 4325376 | tf_op jit(solution)/shard_map/all_gather | solution.py:42
  8.9 285.2 %all-gather.6.cloned.1.call-start = ((), (), s32[]{:S(2)}) async-start(), calls=%async_computation.2 | async-start | bytes 4325376 | tf_op jit(solution)/shard_map/all_gather | solution.py:43
  10.6 441.5 %all-gather.8.cloned.1.call-start = ((), (), s32[]{:S(2)}) async-start(), calls=%async_computation.3 | async-start | bytes 4325376 | tf_op jit(solution)/shard_map/all_gather | solution.py:38
  11.3 1233.2 %all-reduce.3.cloned.1.call-start = ((), (), s32[]{:S(2)}) async-start(), calls=%async_computation.5 | async-start | bytes 33554432
  311.4 2.0 copy-start
  313.6 148.6 %copy-start.2 = (f32[128]{0:T(128)S(1)}, f32[128]{0:T(128)}, u32[]{:S(2)}) copy-start(f32[128]{0:T(128)} %param.7) | copy-start | bytes 1540
  452.1 10.1 copy-start.1
  498.7 0.7 copy-start.3
  498.7 779.3 %reduce-scatter.5.cloned.1.call-start = ((), (), s32[]{:S(2)}) async-start(), calls=%async_computation.4 | async-start | bytes 655360 | tf_op jit(solution)/shard_map/reduce_scatter | solution.py:57
Sparse Core Ops, SparseCore 0:
  9.6 133.4 all-gather.3
  144.6 149.4 all-gather.5
  295.8 156.3 all-gather.7
  498.8 745.6 all-reduce.2
  1247.3 30.7 reduce-scatter.4
where the time goes:
time: 1290 us
  waiting for transfers between devices  1190 us (92%)
  matrix products  40.2 us (3%)
  local copies, waits for them, and re-layouts  37.2 us (3%)
  between operations  13.9 us (1%)
    unnamed x6, waiting for transfers between devices  745 us
    all_gather x1, waiting for transfers between devices, shards(): lax.all_gather(probe_v, 'fsdp', axis=0, tiled=True)  146 us
    all_gather x1, waiting for transfers between devices, shards(): lax.all_gather(k_weight, 'fsdp', axis=0, tiled=True)  139 us
    all_gather x1, waiting for transfers between devices, shards(): lax.all_gather(probe_k, 'fsdp', axis=0, tiled=True)  131 us
    reduce_scatter x1, waiting for transfers between devices, shards(): reduced = lax.psum_scatter(reduced, 'dp', scatter_dimension=0, tiled=True)  30.9 us
  transfers between devices with their start and end apart: 5, of which 5 were waited for; matrix products, arithmetic and copies ran while one was open for 2% of the time, Pallas kernels for 0%

commit v1 on v0

v1 whole, which is shorter than its diff:
```python
import jax
import jax.numpy as jnp
from jax import lax
from jax.experimental import pallas as pl
from jax.experimental.pallas import tpu as pltpu
from jax.sharding import PartitionSpec as P

HEAD = 128
EPS = 1e-06
MESH = pl.DeviceIdType.MESH
F32 = jnp.float32
BF16 = jnp.bfloat16
TOKENS = 131072
ROWS = 1024
COLS = 3 * HEAD
NT = (((1,), (1,)), ((), ()))
N_REMOTE = 30 + 8 + 4 * (6 + 3 + 3) + 4


class Place:
    def __init__(self):
        dp, fs = lax.axis_index("dp"), lax.axis_index("fsdp")
        self.c = dp % 2
        x, z = fs // 8, (fs // 2) % 4
        self.at = {
            "a": x + self.c * (z - x),
            "b": z + self.c * (x - z),
            "y": (dp // 2) * 2 + fs % 2,
        }
        self.fs = fs
        self.y_hi = dp // 2
        self.y_lo = fs % 2

    def xz(self, a, b):
        return a + self.c * (b - a), b + self.c * (a - b)

    def device(self, axis, step):
        at = dict(self.at)
        at[axis] = (at[axis] + step) % 4
        x, z = self.xz(at["a"], at["b"])
        return ((at["y"] // 2) * 2 + self.c, x * 8 + z * 2 + at["y"] % 2)

    def sibling(self):
        return (self.y_hi * 2 + 1 - self.c, self.fs)

    def shard(self, a, b, y_lo):
        x, z = self.xz(a, b)
        return x * 8 + z * 2 + y_lo

    def block(self, a, b, y, core):
        x, z = self.xz(a, b)
        return ((y // 2) * 2 + core) * 32 + x * 8 + z * 2 + y % 2


def kernel(
    normed, kw, gain, pk, pv, out_k, out_v,
    stage, xt, wt, acc, cot, part, r1, r2, r3, probes, result, landed, gcol,
    load_sem, send_sem, recv_sem,
):
    me = Place()
    a, b, y, yl, c = me.at["a"], me.at["b"], me.at["y"], me.y_lo, me.c
    count = [0]
    started = []

    def send(src, dst, device):
        k = count[0]
        count[0] += 1
        copy = pltpu.make_async_remote_copy(
            src_ref=src, dst_ref=dst, send_sem=send_sem.at[k], recv_sem=recv_sem.at[k],
            device_id=device, device_id_type=MESH,
        )
        copy.start()
        started.append(copy)
        return copy

    def same(ref, device):
        return send(ref, ref, device)

    def load(i):
        return pltpu.make_async_copy(
            normed.at[:, pl.ds(i * 512, 512)], stage.at[i % 4], load_sem.at[i % 4]
        )

    barrier = pltpu.get_barrier_semaphore()
    greeted = [me.device(axis, d) for axis in ("a", "b", "y") for d in (1, 2, 3)]
    greeted.append(me.sibling())
    for device in greeted:
        pl.semaphore_signal(barrier, inc=1, device_id=device, device_id_type=MESH)
    loads = [load(i) for i in range(8)]
    for i in range(4):
        loads[i].start()

    for h in range(2):
        cols = pl.ds(pl.multiple_of(c * 256 + h * HEAD, HEAD), HEAD)
        for j, ref in enumerate((kw, pk, pv)):
            wt[h, a, b, yl, j * HEAD:(j + 1) * HEAD, :] = ref[:, cols].T
    gcol[...] = jnp.broadcast_to(gain[...], (HEAD, HEAD)).T
    pl.semaphore_wait(barrier, len(greeted))

    h0, h1 = pl.ds(0, COLS // 2), pl.ds(COLS // 2, COLS // 2)
    am, ap, bm, bp = (a + 3) % 4, (a + 1) % 4, (b + 3) % 4, (b + 1) % 4
    ao, bo, yo = (a + 2) % 4, (b + 2) % 4, 1 - yl
    to = {(axis, d): me.device(axis, d) for axis in ("a", "b", "y") for d in (1, 2, 3)}
    AP, AM, BP, BM, YP, YM = (to[k] for k in (("a", 1), ("a", 3), ("b", 1), ("b", 3), ("y", 1), ("y", 3)))

    c0p, c0m = same(wt.at[0, a, b, yl], AP), same(wt.at[0, a, b, yl], AM)
    d0p, d0m = same(wt.at[1, a, b, yl], BP), same(wt.at[1, a, b, yl], BM)

    sibling = me.sibling()
    pair = []

    def turn(i):
        loads[i].wait()
        for j in range(4):
            k = i * 16 + j * 4
            xt[0, k:k + 4] = stage[i % 4, :, j * HEAD:(j + 1) * HEAD].T.reshape(4, 32, ROWS)
        if i + 4 < 8:
            loads[i + 4].start()
        pair.append(send(xt.at[0, pl.ds(i * 16, 16)], xt.at[1, pl.ds(i * 16, 16)], sibling))

    for i in range(4):
        turn(i)
    c0p.wait_recv()
    f0p = same(wt.at[0, am, b, yl, h0], AP)
    c0m.wait_recv()
    f0m = same(wt.at[0, ap, b, yl, h1], AM)
    d0p.wait_recv()
    g0p = same(wt.at[1, a, bm, yl, h0], BP)
    d0m.wait_recv()
    g0m = same(wt.at[1, a, bp, yl, h1], BM)
    for i in range(4, 8):
        turn(i)

    def over_y(h, b_at):
        return (same(wt.at[h, :, b_at, yl, h0], YP), same(wt.at[h, :, b_at, yl, h1], YM))

    f0p.wait_recv()
    f0m.wait_recv()
    c1p, c1m = same(wt.at[0, :, b, yl], BP), same(wt.at[0, :, b, yl], BM)
    g0p.wait_recv()
    g0m.wait_recv()
    e0p, e0m = same(wt.at[1, a, :, yl, h0], YP), same(wt.at[1, a, :, yl, h1], YM)
    s0p, s0m = same(wt.at[1, a, :, yl], AP), same(wt.at[1, a, :, yl], AM)
    y0 = over_y(0, b)

    def piece(h, halves, shards, first=False):
        @pl.loop(0, 2 * len(halves))
        def _(n):
            half = n // 2 if len(halves) == 2 else halves[0]
            at = pl.ds(pl.multiple_of((n % 2) * 512, 512), 512)
            lhs = jnp.concatenate([wt[h, i, j, k] for i, j, k in shards], axis=1)
            rhs = jnp.concatenate(
                [xt[half, pl.ds(4 * me.shard(i, j, k), 4), :, at].reshape(HEAD, 512) for i, j, k in shards], axis=0
            )
            new = jnp.dot(lhs, rhs, preferred_element_type=F32)
            if first:
                acc[h, half, :, at] = new
            else:
                acc[h, half, :, at] += new

    every = range(4)
    piece(0, (0,), [(i, b, yl) for i in every], first=True)
    piece(1, (0,), [(a, j, yl) for j in every], first=True)
    e0p.wait_recv()
    e0m.wait_recv()
    s1p, s1m = same(wt.at[1, a, :, yo], AP), same(wt.at[1, a, :, yo], AM)
    piece(1, (0,), [(a, j, yo) for j in every])
    c1p.wait_recv()
    f1p = same(wt.at[0, :, bm, yl, h0], BP)
    y1 = over_y(0, bm)
    c1m.wait_recv()
    f1m = same(wt.at[0, :, bp, yl, h1], BM)
    y2 = over_y(0, bp)
    for copy in y0:
        copy.wait_recv()
    piece(0, (0,), [(i, b, yo) for i in every])
    s0p.wait_recv()
    t0p = same(wt.at[1, am, :, yl, h0], AP)
    s0m.wait_recv()
    t0m = same(wt.at[1, ap, :, yl, h1], AM)
    piece(1, (0,), [(i, j, yl) for i in (am, ap) for j in every])
    f1p.wait_recv()
    f1m.wait_recv()
    y3 = over_y(0, bo)
    piece(0, (0,), [(i, j, yl) for i in every for j in (bm, bp)])
    s1p.wait_recv()
    t1p = same(wt.at[1, am, :, yo, h0], AP)
    s1m.wait_recv()
    t1m = same(wt.at[1, ap, :, yo, h1], AM)
    for copy in pair:
        copy.wait_recv()
    piece(1, (1,), [(a, j, k) for j in every for k in (yl, yo)]
          + [(i, j, yl) for i in (am, ap) for j in every], first=True)
    piece(0, (1,), [(i, b, k) for i in every for k in (yl, yo)]
          + [(i, j, yl) for i in every for j in (bm, bp)], first=True)
    piece(1, (0, 1), [(i, j, yo) for i in (am, ap) for j in every])
    for copy in y1 + y2:
        copy.wait_recv()
    piece(0, (0, 1), [(i, j, yo) for i in every for j in (bm, bp)])
    for copy in (t0p, t0m, t1p, t1m):
        copy.wait_recv()
    piece(1, (0, 1), [(ao, j, k) for j in every for k in (yl, yo)])
    for copy in y3:
        copy.wait_recv()
    piece(0, (0, 1), [(i, bo, k) for i in every for k in (yl, yo)])

    for h in range(2):
        for half in range(2):
            cot[h * HEAD:(h + 1) * HEAD, half * ROWS:(half + 1) * ROWS] = (
                acc[h, half, 2 * HEAD:3 * HEAD, :].astype(BF16)
            )

    def cot_k(h):
        @pl.loop(0, 16)
        def _(n):
            half = n // 8
            at = pl.ds(pl.multiple_of((n % 8) * HEAD, HEAD), HEAD)
            alpha = acc[h, half, 0:HEAD, at]
            delta = acc[h, half, HEAD:2 * HEAD, at]
            g = gcol[...]
            inv = lax.rsqrt(jnp.mean(alpha * alpha, axis=0, keepdims=True) + EPS)
            cubed = inv * inv * inv
            along = jnp.sum(alpha * delta, axis=0, keepdims=True) / HEAD
            gt = g * (g * (delta * inv - alpha * (along * cubed)))
            back = gt * inv - alpha * ((jnp.sum(alpha * gt, axis=0, keepdims=True) / HEAD) * cubed)
            cot[(2 + h) * HEAD:(3 + h) * HEAD, pl.ds(pl.multiple_of(n * HEAD, HEAD), HEAD)] = back.astype(BF16)

    axes = (("a", "y", "b"), ("y", "a", "b"), ("b", "y", "a"), ("a", "y", "b"))
    first = [{} for _ in axes]

    def spot(q, at):
        i, j, k = (at[axis] for axis in axes[q])
        return i * 16 + j * 4 + k

    def tile(pair_at, at1, at2, i1, i2):
        third = next(axis for axis in ("a", "b", "y") if axis not in (at1, at2))
        spots = [{at1: i1, at2: i2, third: k} for k in every]
        blocks = [me.block(s["a"], s["b"], s["y"], core) for s in spots for core in range(2)]
        lhs = jnp.concatenate(
            [jnp.concatenate([xt[half, k] for k in blocks], axis=0) for half in range(2)], axis=1
        )
        new = lax.dot_general(
            lhs, cot[pl.ds(pair_at * 2 * HEAD, 2 * HEAD), :], NT, preferred_element_type=F32
        )
        for n, s in enumerate(spots):
            for q in range(2):
                part[2 * pair_at + q, spot(2 * pair_at + q, s)] = (
                    new[n * 64:(n + 1) * 64, q * HEAD:(q + 1) * HEAD]
                )

    def half_of(q, step, half):
        return part.at[q, pl.ds(((me.at[axes[q][0]] + step) % 4) * 16 + half * 8, 8)]

    def far(q):
        axis = axes[q][0]
        first[q][0] = send(half_of(q, 2, 0), r1.at[q, 0], to[axis, 1])
        first[q][1] = send(half_of(q, 2, 1), r1.at[q, 1], to[axis, 3])

    def near_plus(q):
        first[q][2] = send(half_of(q, 1, 1), r1.at[q, 2], to[axes[q][0], 1])

    def near_minus(q):
        first[q][3] = send(half_of(q, 3, 0), r1.at[q, 3], to[axes[q][0], 3])

    def add(q, step, half, slots):
        base = ((me.at[axes[q][0]] + step) % 4) * 16 + half * 8
        for slot in slots:
            first[q][slot].wait_recv()

        @pl.loop(0, 8)
        def _(n):
            total = part[q, base + n]
            for slot in slots:
                total = total + r1[q, slot, n]
            part[q, base + n] = total

    def relay(q):
        axis = axes[q][0]
        add(q, 1, 0, (0,))
        first[q][4] = send(half_of(q, 1, 0), r1.at[q, 4], to[axis, 1])
        add(q, 3, 1, (1,))
        first[q][5] = send(half_of(q, 3, 1), r1.at[q, 5], to[axis, 3])

    def product(pair_at, q1, q2):
        at1, at2 = axes[q1][0], axes[q2][0]
        m1, m2 = me.at[at1], me.at[at2]

        @pl.loop(0, 4)
        def _(n):
            tile(pair_at, at1, at2, (m1 + 2) % 4, (m2 + 2 + n) % 4)

        far(q1)

        @pl.loop(0, 3)
        def _(n):
            tile(pair_at, at1, at2, (m1 + 3 + n) % 4, (m2 + 2) % 4)

        far(q2)

        @pl.loop(0, 3)
        def _(n):
            tile(pair_at, at1, at2, (m1 + 1) % 4, (m2 + 3 + n) % 4)

        near_plus(q1)

        @pl.loop(0, 3)
        def _(n):
            tile(pair_at, at1, at2, (m1 + 3) % 4, (m2 + 3 + n) % 4)

        near_minus(q1)

        @pl.loop(0, 3)
        def _(n):
            tile(pair_at, at1, at2, m1, (m2 + 3 + n) % 4)

        near_plus(q2)
        near_minus(q2)

    def second(q):
        add(q, 0, 0, (3, 4))
        add(q, 0, 1, (2, 5))
        i, j = me.at[axes[q][0]], me.at[axes[q][1]]
        return [
            send(part.at[q, pl.ds(i * 16 + ((j + d) % 4) * 4, 4)], r2.at[q, d - 1], to[axes[q][1], d])
            for d in (2, 1, 3)
        ]

    def third(q, copies):
        i, j, k = (me.at[axis] for axis in axes[q])
        for copy in copies:
            copy.wait_recv()
        base = i * 16 + j * 4

        @pl.loop(0, 4)
        def _(n):
            part[q, base + n] = part[q, base + n] + r2[q, 0, n] + r2[q, 1, n] + r2[q, 2, n]

        return [
            send(part.at[q, base + (k + d) % 4], r3.at[q, d - 1], to[axes[q][2], d]) for d in (2, 1, 3)
        ]

    def last(q, copies):
        for copy in copies:
            copy.wait_recv()
        total = part[q, spot(q, me.at)] + r3[q, 0] + r3[q, 1] + r3[q, 2]
        result[q] = (total * probes[q]) * (1.0 / TOKENS)
        return send(result.at[q, pl.ds(pl.multiple_of((1 - c) * 32, 32), 32)], landed.at[q], sibling)

    product(0, 0, 1)
    cot_k(0)
    cot_k(1)
    relay(0)
    relay(1)
    product(1, 3, 2)
    relay(3)
    relay(2)

    for core in range(2):
        s = (me.y_hi * 2 + core) * 8 + me.fs // 4
        i, j = me.xz(s // 8, (s // 2) % 4)
        for q in range(4):
            h, row = q % 2, (2 * HEAD if q < 2 else HEAD)
            gcol[...] = wt[h, i, j, s % 2, row:row + HEAD, :].T.astype(F32)
            probes[q, core * 32:(core + 1) * 32] = gcol[pl.ds(pl.multiple_of((me.fs % 4) * 32, 32), 32), :]

    s = [None] * 4
    t = [None] * 4
    for q in (0, 1, 3, 2):
        s[q] = second(q)
    for q in (0, 1, 3, 2):
        t[q] = third(q, s[q])
    final = [None] * 4
    for q in (0, 1, 3, 2):
        final[q] = last(q, t[q])
    for q in range(4):
        out = out_v if q < 2 else out_k
        mine = pl.ds(pl.multiple_of(c * 256 + (q % 2) * HEAD, HEAD), HEAD)
        theirs = pl.ds(pl.multiple_of((1 - c) * 256 + (q % 2) * HEAD, HEAD), HEAD)
        out[:, mine] = result[q, pl.ds(pl.multiple_of(c * 32, 32), 32), :]
        final[q].wait_recv()
        out[:, theirs] = landed[q]
    for copy in started:
        copy.wait_send()
    assert count[0] == N_REMOTE


def shards(normed, k_weight, k_gain, probe_k, probe_v):
    vmem = pl.BlockSpec(memory_space=pltpu.VMEM)
    out = jax.ShapeDtypeStruct((32, 512), F32)
    return pl.pallas_call(
        kernel,
        name="curvature",
        out_shape=(out, out),
        in_specs=[pl.BlockSpec(memory_space=pl.ANY)] + [vmem] * 4,
        out_specs=(vmem, vmem),
        scratch_shapes=[
            pltpu.VMEM((4, ROWS, 512), BF16),
            pltpu.VMEM((2, 128, 32, ROWS), BF16),
            pltpu.VMEM((2, 4, 4, 2, COLS, HEAD), BF16),
            pltpu.VMEM((2, 2, COLS, ROWS), F32),
            pltpu.VMEM((4 * HEAD, 2 * ROWS), BF16),
            pltpu.VMEM((4, 64, 64, HEAD), F32),
            pltpu.VMEM((4, 6, 8, 64, HEAD), F32),
            pltpu.VMEM((4, 3, 4, 64, HEAD), F32),
            pltpu.VMEM((4, 3, 64, HEAD), F32),
            pltpu.VMEM((4, 64, HEAD), F32),
            pltpu.VMEM((4, 64, HEAD), F32),
            pltpu.VMEM((4, 32, HEAD), F32),
            pltpu.VMEM((HEAD, HEAD), F32),
            pltpu.SemaphoreType.DMA((4,)),
            pltpu.SemaphoreType.DMA((N_REMOTE,)),
            pltpu.SemaphoreType.DMA((N_REMOTE,)),
        ],
        compiler_params=pltpu.CompilerParams(
            collective_id=0, has_side_effects=True, vmem_limit_bytes=58 * 2**20
        ),
        cost_estimate=pl.CostEstimate(flops=21 * 10**9, bytes_accessed=10**7, transcendentals=0),
    )(normed, k_weight, k_gain.reshape(1, HEAD), probe_k, probe_v)


def solution(mesh):
    return jax.shard_map(
        shards,
        mesh=mesh,
        in_specs=(P(("dp", "fsdp"), None), P("fsdp", None), P(), P("fsdp", None), P("fsdp", None)),
        out_specs=(P(("dp", "fsdp"), None), P(("dp", "fsdp"), None)),
        check_vma=False,
    )
```

time: 1290 us -> 103 us (0.08)
  waiting for transfers between devices: 1190 us -> 0 us
  Pallas kernels: 0 us -> 98.8 us
  matrix products: 40.2 us -> 0 us
  local copies, waits for them, and re-layouts: 37.2 us -> 2.95 us
  between operations: 13.9 us -> 0.64 us
    unnamed x6 -> x0, waiting for transfers between devices: 745 us -> none
    all_gather x3 -> x0, waiting for transfers between devices: 416 us -> none  [the longest x1 146 us: shards(): lax.all_gather(probe_v, 'fsdp', axis=0, tiled=True)]
    pallas_call x0 -> x1, Pallas kernels: none -> 98.8 us  [shards(): pl.pallas_call(kernel, name='curvature', out_shape=(out, out), in_specs=[...]
    dot_general x3 -> x0, matrix products: 40.2 us -> none  [the longest x1 17.5 us: shards(): lax.dot_general(normed, cot, (((0,), (0,)), ((), ())), preferred_element_...]
    reduce_scatter x1 -> x0, waiting for transfers between devices: 30.9 us -> none  [shards(): reduced = lax.psum_scatter(reduced, 'dp', scatter_dimension=0, tiled=True)]
    mul x2 -> x0, local copies, waits for them, and re-layouts: 18.1 us -> none  [the longest x1 17.4 us: shards(): term = term * probes.astype(jnp.float32)]
  transfers between devices with their start and end apart: 5 -> 0, of which waited for: 5 -> 0; matrix products, arithmetic and copies ran while one was open for 2% -> 0% of each run, Pallas kernels for 0% -> 0%
where the time goes in v1:
time: 103 us; the launch traced here: 102 us
  Pallas kernels  98.8 us (96%)
  local copies, waits for them, and re-layouts  2.95 us (3%)
    pallas_call x1, Pallas kernels, shards(): pl.pallas_call(kernel, name='curvature', out_shape=(out, out), in_specs=[...  98.8 us
    unnamed x2, local copies, waits for them, and re-layouts  2.95 us

profile of v1, /device:TPU:1, one launch (start us, length us, event | category | flops | bytes accessed | tf_op | source)
XLA Modules:
  0.0 102.4 jit_solution(1868137911587333788)
XLA Ops:
  0.6 98.8 %curvature.1 = (f32[32,512]{1,0:T(8,128)}, f32[32,512]{1,0:T(8,128)}) custom-call(bf16[1024,4096]{1,0:T(8,128)(2,1)} %normed.1, bf16[128,512]{1,0:T(8,128)(2,1)} %kw.1, f32[1,128]{1,0:T(1,128)} %bitcast.1, bf16[128,512]{1,0:T(8,128)(2,1)} %pk.1, bf16[128,512]{1,0:T(8,128)(2,1)} %pv.1), custom_call_target="tpu_custom_call" | custom-call | flops 20999999488 | bytes 10000000 | tf_op jit(solution)/shard_map/curvature/pallas_call | solution.py:390
  99.5 1.5 %copy.9 = f32[32,512]{1,0:T(8,128)} copy(f32[32,512]{1,0:T(8,128)} %get-tuple-element.4) | data formatting | bytes 131072
  100.9 1.5 %copy.10 = f32[32,512]{1,0:T(8,128)} copy(f32[32,512]{1,0:T(8,128)} %get-tuple-element.5) | data formatting | bytes 131072

commit v2 on v1

v2 whole, which is shorter than its diff:
```python
import jax
import jax.numpy as jnp
from jax import lax
from jax.experimental import pallas as pl
from jax.experimental.pallas import tpu as pltpu
from jax.sharding import PartitionSpec as P

HEAD = 128
EPS = 1e-06
MESH = pl.DeviceIdType.MESH
F32 = jnp.float32
BF16 = jnp.bfloat16
TOKENS = 131072
ROWS = 1024
NT = (((1,), (1,)), ((), ()))
N_REMOTE = 56 + 8 + 4 * (6 + 3 + 3) + 4


class Place:
    def __init__(self):
        dp, fs = lax.axis_index("dp"), lax.axis_index("fsdp")
        self.c = dp % 2
        x, z = fs // 8, (fs // 2) % 4
        self.at = {
            "a": x + self.c * (z - x),
            "b": z + self.c * (x - z),
            "y": (dp // 2) * 2 + fs % 2,
        }
        self.fs = fs
        self.y_hi = dp // 2
        self.y_lo = fs % 2

        self.sa, self.sb = 8 - 6 * self.c, 2 + 6 * self.c

    def xz(self, a, b):
        return a + self.c * (b - a), b + self.c * (a - b)

    def device(self, axis, step):
        at = dict(self.at)
        at[axis] = (at[axis] + step) % 4
        x, z = self.xz(at["a"], at["b"])
        return ((at["y"] // 2) * 2 + self.c, x * 8 + z * 2 + at["y"] % 2)

    def sibling(self):
        return (self.y_hi * 2 + 1 - self.c, self.fs)

    def shard(self, a, b, y_lo):
        return a * self.sa + b * self.sb + y_lo

    def block(self, a, b, y, core):
        return a * self.sa + b * self.sb + ((y // 2) * 64 + y % 2) + core * 32


GROUP = 32
MIDDLE = 15500 / 128
SHIFT = 121.0


def encode(x, ref):
    groups = x.shape[0] // GROUP
    x = x.reshape(groups, GROUP, HEAD)
    top = jnp.maximum(jnp.max(jnp.abs(x), axis=1) * 1.01, 1e-30).astype(BF16)
    steps = MIDDLE / top.astype(F32)
    u = x * steps[:, None, :] + MIDDLE
    k = jnp.floor(u)
    code = (jnp.exp2(k - SHIFT) * (1.0 + (u - k))).astype(BF16)
    ref[0:groups * GROUP, :] = code.reshape(groups * GROUP, HEAD)
    if groups < 16:
        top = jnp.concatenate([top.astype(F32), jnp.zeros((16 - groups, HEAD), F32)], axis=0).astype(BF16)
    ref[groups * GROUP:groups * GROUP + 16, :] = top


def decode(ref, rows):
    groups = rows // GROUP
    y = ref[0:rows, :].astype(F32).reshape(groups, GROUP, HEAD)
    top = ref[rows:rows + 16, :].astype(F32)[0:groups] * (1.0 / MIDDLE)
    k = jnp.floor(jnp.log2(y * (1.0 + 1.0 / 512.0)))
    u = (k + (SHIFT - 1.0 - MIDDLE)) + y * jnp.exp2(-k)
    return (u * top[:, None, :]).reshape(rows, HEAD)


def kernel(
    normed, kw, gain, pk, pv, out_k, out_v,
    stage, xt, wk, wv, acc, cot, part, o1, r1, o2, r2, r3, probes, result, landed, gcol,
    load_sem, send_sem, recv_sem,
):
    me = Place()
    a, b, yl, c = me.at["a"], me.at["b"], me.y_lo, me.c
    every = range(4)
    count = [0]
    started = []

    def send(src, dst, device, now=True):
        k = count[0]
        count[0] += 1
        copy = pltpu.make_async_remote_copy(
            src_ref=src, dst_ref=dst, send_sem=send_sem.at[k], recv_sem=recv_sem.at[k],
            device_id=device, device_id_type=MESH,
        )
        started.append(copy)
        if now:
            copy.start()
        return copy

    def same(ref, device):
        return send(ref, ref, device)

    def arrive(*copies):
        for copy in copies:
            copy.wait_recv()

    def load(i):
        return pltpu.make_async_copy(
            normed.at[:, pl.ds(i * 512, 512)], stage.at[i % 4], load_sem.at[i % 4]
        )

    barrier = pltpu.get_barrier_semaphore()
    greeted = [me.device(axis, d) for axis in ("a", "b", "y") for d in (1, 2, 3)]
    greeted.append(me.sibling())
    for device in greeted:
        pl.semaphore_signal(barrier, inc=1, device_id=device, device_id_type=MESH)
    loads = [load(i) for i in range(8)]
    for i in range(4):
        loads[i].start()

    to = {(axis, d): me.device(axis, d) for axis in ("a", "b", "y") for d in (1, 2, 3)}
    AP, AM, BP, BM, YP, YM = (to[k] for k in (("a", 1), ("a", 3), ("b", 1), ("b", 3), ("y", 1), ("y", 3)))
    am, ap, bm, bp = (a + 3) % 4, (a + 1) % 4, (b + 3) % 4, (b + 1) % 4
    ao, bo, yo = (a + 2) % 4, (b + 2) % 4, 1 - yl
    sibling = me.sibling()

    class Gather:
        def __init__(self, w, rows):
            self.w = w
            self.h0, self.h1 = pl.ds(0, rows // 2), pl.ds(rows // 2, rows // 2)

        def over_y(self, at):
            w = self.w
            return same(w.at[0, :, at, yl, self.h0], YP), same(w.at[0, :, at, yl, self.h1], YM)

        def start(self):
            w = self.w
            self.c0 = [same(w.at[0, a, b, yl], to["a", d]) for d in (2, 1, 3)]
            self.d0 = [same(w.at[1, a, b, yl], to["b", d]) for d in (2, 1, 3)]

        def second(self):
            w = self.w
            arrive(*self.c0)
            self.c1 = same(w.at[0, :, b, yl], BP), same(w.at[0, :, b, yl], BM)
            arrive(*self.d0)
            self.e0 = same(w.at[1, a, :, yl, self.h0], YP), same(w.at[1, a, :, yl, self.h1], YM)
            self.y0 = self.over_y(b)
            self.s0 = same(w.at[1, a, :, yl], AP), same(w.at[1, a, :, yl], AM)

        def after_e0(self):
            w = self.w
            arrive(*self.e0)
            self.s1 = same(w.at[1, a, :, yo], AP), same(w.at[1, a, :, yo], AM)

        def after_c1(self):
            w = self.w
            arrive(self.c1[0])
            f0 = same(w.at[0, :, bm, yl, self.h0], BP)
            arrive(self.c1[1])
            f1 = same(w.at[0, :, bp, yl, self.h1], BM)
            self.f1 = f0, f1
            self.y1 = self.over_y(bm) + self.over_y(bp)

        def after_s(self, k):
            w = self.w
            copies, at = (self.s0, yl) if k == 0 else (self.s1, yo)
            arrive(copies[0])
            t0 = same(w.at[1, am, :, at, self.h0], AP)
            arrive(copies[1])
            t1 = same(w.at[1, ap, :, at, self.h1], AM)
            if k == 0:
                self.t0 = t0, t1
            else:
                self.t1 = t0, t1

        def after_f1(self):
            arrive(*self.f1)
            self.y2 = self.over_y(bo)

    keys, values = Gather(wk, 2 * HEAD), Gather(wv, HEAD)

    for h in range(2):
        cols = pl.ds(pl.multiple_of(c * 256 + h * HEAD, HEAD), HEAD)
        wk[h, a, b, yl, 0:HEAD, :] = kw[:, cols].T
        wk[h, a, b, yl, HEAD:2 * HEAD, :] = pk[:, cols].T
    pl.semaphore_wait(barrier, len(greeted))
    keys.start()

    pair = []

    def turn(i):
        loads[i].wait()
        for j in range(4):
            k = i * 16 + j * 4
            xt[0, k:k + 4] = stage[i % 4, :, j * HEAD:(j + 1) * HEAD].T.reshape(4, 32, ROWS)
        if i + 4 < 8:
            loads[i + 4].start()
        pair.append(send(xt.at[0, pl.ds(i * 16, 16)], xt.at[1, pl.ds(i * 16, 16)], sibling))

    for h in range(2):
        cols = pl.ds(pl.multiple_of(c * 256 + h * HEAD, HEAD), HEAD)
        wv[h, a, b, yl] = pv[:, cols].T
    gcol[...] = jnp.broadcast_to(gain[...], (HEAD, HEAD)).T
    for i in range(4):
        turn(i)
    keys.second()
    values.start()
    for i in range(4, 8):
        turn(i)

    def piece(h, halves, shards, first=False):
        @pl.loop(0, 2 * len(halves))
        def _(n):
            half = n // 2 if len(halves) == 2 else halves[0]
            at = pl.ds(pl.multiple_of((n % 2) * 512, 512), 512)
            lhs = jnp.concatenate([wk[h, i, j, k] for i, j, k in shards], axis=1)
            rhs = jnp.concatenate(
                [xt[half, pl.ds(4 * me.shard(i, j, k), 4), :, at].reshape(HEAD, 512) for i, j, k in shards], axis=0
            )
            new = jnp.dot(lhs, rhs, preferred_element_type=F32)
            if first:
                acc[h, half, :, at] = new
            else:
                acc[h, half, :, at] += new

    piece(0, (0,), [(i, b, yl) for i in every], first=True)
    piece(1, (0,), [(a, j, yl) for j in every], first=True)
    keys.after_e0()
    keys.after_c1()
    values.second()
    keys.after_s(0)
    piece(1, (0,), [(a, j, yo) for j in every])
    arrive(*keys.y0)
    piece(0, (0,), [(i, b, yo) for i in every])
    keys.after_f1()
    keys.after_s(1)
    values.after_e0()
    values.after_c1()
    piece(1, (0,), [(i, j, yl) for i in (am, ap) for j in every])
    piece(0, (0,), [(i, j, yl) for i in every for j in (bm, bp)])
    arrive(*pair)
    piece(1, (1,), [(a, j, k) for j in every for k in (yl, yo)]
          + [(i, j, yl) for i in (am, ap) for j in every], first=True)
    values.after_s(0)
    values.after_f1()
    values.after_s(1)
    piece(0, (1,), [(i, b, k) for i in every for k in (yl, yo)]
          + [(i, j, yl) for i in every for j in (bm, bp)], first=True)
    piece(1, (0, 1), [(i, j, yo) for i in (am, ap) for j in every])
    arrive(*keys.y1)
    piece(0, (0, 1), [(i, j, yo) for i in every for j in (bm, bp)])
    arrive(*keys.t0, *keys.t1)
    piece(1, (0, 1), [(ao, j, k) for j in every for k in (yl, yo)])
    arrive(*keys.y2)
    piece(0, (0, 1), [(i, bo, k) for i in every for k in (yl, yo)])

    def cot_k():
        @pl.loop(0, 8)
        def _(n):
            at = pl.ds(pl.multiple_of((n % 4) * 256, 256), 256)
            for h in range(2):
                alpha = acc[h, n // 4, 0:HEAD, at]
                delta = acc[h, n // 4, HEAD:2 * HEAD, at]
                g = jnp.concatenate([gcol[...]] * 2, axis=1)
                inv = lax.rsqrt(jnp.mean(alpha * alpha, axis=0, keepdims=True) + EPS)
                cubed = inv * inv * inv
                along = jnp.sum(alpha * delta, axis=0, keepdims=True) / HEAD
                gt = g * (g * (delta * inv - alpha * (along * cubed)))
                back = gt * inv - alpha * ((jnp.sum(alpha * gt, axis=0, keepdims=True) / HEAD) * cubed)
                cot[(2 + h) * HEAD:(3 + h) * HEAD, pl.ds(pl.multiple_of(n * 256, 256), 256)] = back.astype(BF16)

    def cot_v():
        @pl.loop(0, 4)
        def _(n):
            lhs = jnp.concatenate(
                [
                    jnp.concatenate([wv[h, i, j, k] for s in range(16) for i, j in (me.xz(s // 4, s % 4),) for k in range(2)], axis=1)
                    for h in range(2)
                ],
                axis=0,
            )
            rhs = xt[n // 2, :, :, pl.ds(pl.multiple_of((n % 2) * 512, 512), 512)].reshape(32 * HEAD, 512)
            new = jnp.dot(lhs, rhs, preferred_element_type=F32)
            cot[0:2 * HEAD, pl.ds(pl.multiple_of(n * 512, 512), 512)] = new.astype(BF16)

    axes = (("a", "y", "b"), ("a", "b", "y"), ("a", "y", "b"), ("y", "a", "b"))
    first = [{} for _ in axes]

    def spot(q, at):
        i, j, k = (at[axis] for axis in axes[q])
        return i * 16 + j * 4 + k

    def tile(q1, q2, i1):
        spots = [dict(zip(axes[q1], (i1, j, k))) for j in every for k in every]
        blocks = [me.block(s["a"], s["b"], s["y"], core) for s in spots for core in range(2)]
        lhs = jnp.concatenate(
            [jnp.concatenate([xt[half, k] for k in blocks], axis=0) for half in range(2)], axis=1
        )
        low = min(q1, q2)
        new = lax.dot_general(lhs, cot[low * HEAD:(low + 2) * HEAD, :], NT, preferred_element_type=F32)
        for n, s in enumerate(spots):
            for q in (low, low + 1):
                part[q, spot(q, s)] = new[n * 64:(n + 1) * 64, (q - low) * HEAD:(q - low + 1) * HEAD]

    def base(q, step, half):
        return ((me.at[axes[q][0]] + step) % 4) * 16 + half * 8

    plan = ((2, 0, 1), (2, 1, 3), (1, 1, 1), (3, 0, 3), (1, 0, 1), (3, 1, 3))

    def ready(q):
        for slot, (step, half, way) in enumerate(plan):
            first[q][slot] = send(o1.at[q, slot], r1.at[q, slot], to[axes[q][0], way], now=False)

    def ship(q, slot, incoming=None):
        step, half, way = plan[slot]
        x = part[q, pl.ds(base(q, step, half), 8)].reshape(512, HEAD)
        if incoming is not None:
            x = x + decode(r1.at[q, incoming], 512)
        encode(x, o1.at[q, slot])
        first[q][slot].start()

    def product(q1, q2):
        ready(q1)
        ready(q2)
        mine = me.at[axes[q1][0]]
        along = (q1, q2) if axes[q1][0] == axes[q2][0] else (q1,)

        @pl.loop(0, 4)
        def _(n):
            tile(q1, q2, (mine + 2 + 3 * n + (n // 2) * (3 + 2 * (n % 2))) % 4)

            @pl.when(n == 0)
            def _():
                for q in along:
                    ship(q, 0)
                    ship(q, 1)

            @pl.when(n == 1)
            def _():
                for q in along:
                    ship(q, 2)

            @pl.when(n == 2)
            def _():
                for q in along:
                    ship(q, 3)

        if len(along) == 1:
            for slot in range(4):
                ship(q2, slot)

    def relay(q):
        first[q][0].wait_recv()
        ship(q, 4, 0)
        first[q][1].wait_recv()
        ship(q, 5, 1)

    s = [None] * 4
    t = [None] * 4
    final = [None] * 4

    def second(q):
        for half, slots in ((0, (3, 4)), (1, (2, 5))):
            at = pl.ds(base(q, 0, half), 8)
            total = part[q, at].reshape(512, HEAD)
            for slot in slots:
                first[q][slot].wait_recv()
                total = total + decode(r1.at[q, slot], 512)
            part[q, at] = total.reshape(8, 64, HEAD)
        i, j = me.at[axes[q][0]], me.at[axes[q][1]]
        s[q] = []
        for d in (2, 1, 3):
            encode(part[q, pl.ds(i * 16 + ((j + d) % 4) * 4, 4)].reshape(256, HEAD), o2.at[q, d - 1])
            s[q].append(send(o2.at[q, d - 1], r2.at[q, d - 1], to[axes[q][1], d]))

    def third(q):
        i, j, k = (me.at[axis] for axis in axes[q])
        at = pl.ds(i * 16 + j * 4, 4)
        total = part[q, at].reshape(256, HEAD)
        for n, d in enumerate((2, 1, 3)):
            s[q][n].wait_recv()
            total = total + decode(r2.at[q, d - 1], 256)
        part[q, at] = total.reshape(4, 64, HEAD)
        t[q] = [
            send(part.at[q, i * 16 + j * 4 + (k + d) % 4], r3.at[q, d - 1], to[axes[q][2], d]) for d in (2, 1, 3)
        ]

    def last(q):
        arrive(*t[q])
        total = part[q, spot(q, me.at)] + r3[q, 0] + r3[q, 1] + r3[q, 2]
        result[q] = (total * probes[q]) * (1.0 / TOKENS)
        final[q] = send(result.at[q, pl.ds(pl.multiple_of((1 - c) * 32, 32), 32)], landed.at[q], sibling)

    cot_k()
    product(2, 3)
    arrive(*values.y0, *values.y1, *values.y2, *values.t0, *values.t1)
    cot_v()
    relay(2)
    product(1, 0)
    relay(3)
    second(2)
    relay(1)
    relay(0)

    for core in range(2):
        n = (me.y_hi * 2 + core) * 8 + me.fs // 4
        i, j = me.xz(n // 8, (n // 2) % 4)
        for q in range(4):
            turned = wv[q, i, j, n % 2] if q < 2 else wk[q - 2, i, j, n % 2, HEAD:2 * HEAD, :]
            gcol[...] = turned.T.astype(F32)
            probes[q, core * 32:(core + 1) * 32] = gcol[pl.ds(pl.multiple_of((me.fs % 4) * 32, 32), 32), :]

    second(3)
    third(2)
    second(1)
    second(0)
    third(3)
    last(2)
    third(1)
    third(0)
    last(3)
    last(1)
    last(0)
    for q in range(4):
        out = out_v if q < 2 else out_k
        mine = pl.ds(pl.multiple_of(c * 256 + (q % 2) * HEAD, HEAD), HEAD)
        theirs = pl.ds(pl.multiple_of((1 - c) * 256 + (q % 2) * HEAD, HEAD), HEAD)
        out[:, mine] = result[q, pl.ds(pl.multiple_of(c * 32, 32), 32), :]
        final[q].wait_recv()
        out[:, theirs] = landed[q]
    for copy in started:
        copy.wait_send()
    assert count[0] == N_REMOTE


def shards(normed, k_weight, k_gain, probe_k, probe_v):
    vmem = pl.BlockSpec(memory_space=pltpu.VMEM)
    out = jax.ShapeDtypeStruct((32, 512), F32)
    return pl.pallas_call(
        kernel,
        name="curvature",
        out_shape=(out, out),
        in_specs=[pl.BlockSpec(memory_space=pl.ANY)] + [vmem] * 4,
        out_specs=(vmem, vmem),
        scratch_shapes=[
            pltpu.VMEM((4, ROWS, 512), BF16),
            pltpu.VMEM((2, 128, 32, ROWS), BF16),
            pltpu.VMEM((2, 4, 4, 2, 2 * HEAD, HEAD), BF16),
            pltpu.VMEM((2, 4, 4, 2, HEAD, HEAD), BF16),
            pltpu.VMEM((2, 2, 2 * HEAD, ROWS), F32),
            pltpu.VMEM((4 * HEAD, 2 * ROWS), BF16),
            pltpu.VMEM((4, 64, 64, HEAD), F32),
            pltpu.VMEM((4, 6, 528, HEAD), BF16),
            pltpu.VMEM((4, 6, 528, HEAD), BF16),
            pltpu.VMEM((4, 3, 272, HEAD), BF16),
            pltpu.VMEM((4, 3, 272, HEAD), BF16),
            pltpu.VMEM((4, 3, 64, HEAD), F32),
            pltpu.VMEM((4, 64, HEAD), F32),
            pltpu.VMEM((4, 64, HEAD), F32),
            pltpu.VMEM((4, 32, HEAD), F32),
            pltpu.VMEM((HEAD, HEAD), F32),
            pltpu.SemaphoreType.DMA((4,)),
            pltpu.SemaphoreType.DMA((N_REMOTE,)),
            pltpu.SemaphoreType.DMA((N_REMOTE,)),
        ],
        compiler_params=pltpu.CompilerParams(
            collective_id=0, has_side_effects=True, vmem_limit_bytes=58 * 2**20
        ),
        cost_estimate=pl.CostEstimate(flops=21 * 10**9, bytes_accessed=10**7, transcendentals=0),
    )(normed, k_weight, k_gain.reshape(1, HEAD), probe_k, probe_v)


def solution(mesh):
    return jax.shard_map(
        shards,
        mesh=mesh,
        in_specs=(P(("dp", "fsdp"), None), P("fsdp", None), P(), P("fsdp", None), P("fsdp", None)),
        out_specs=(P(("dp", "fsdp"), None), P(("dp", "fsdp"), None)),
        check_vma=False,
    )
```

time: 103 us -> 91.4 us (0.89)
  Pallas kernels: 98.8 us -> 87.3 us
    pallas_call x1, Pallas kernels: 98.8 us -> 87.3 us  [shards(): pl.pallas_call(kernel, name='curvature', out_shape=(out, out), in_specs=[...]
where the time goes in v2:
time: 91.4 us; the launch traced here: 90.9 us
  Pallas kernels  87.3 us (96%)
  local copies, waits for them, and re-layouts  2.95 us (3%)
    pallas_call x1, Pallas kernels, shards(): pl.pallas_call(kernel, name='curvature', out_shape=(out, out), in_specs=[...  87.3 us
    unnamed x2, local copies, waits for them, and re-layouts  2.95 us

profile of v2, /device:TPU:1, one launch (start us, length us, event | category | flops | bytes accessed | tf_op | source)
XLA Modules:
  0.0 90.9 jit_solution(9759673210906035236)
XLA Ops:
  0.6 87.3 %curvature.1 = (f32[32,512]{1,0:T(8,128)}, f32[32,512]{1,0:T(8,128)}) custom-call(bf16[1024,4096]{1,0:T(8,128)(2,1)} %normed.1, bf16[128,512]{1,0:T(8,128)(2,1)} %kw.1, f32[1,128]{1,0:T(1,128)} %bitcast.1, bf16[128,512]{1,0:T(8,128)(2,1)} %pk.1, bf16[128,512]{1,0:T(8,128)(2,1)} %pv.1), custom_call_target="tpu_custom_call" | custom-call | flops 20999999488 | bytes 10000000 | tf_op jit(solution)/shard_map/curvature/pallas_call | solution.py:444
  87.9 1.5 %copy.9 = f32[32,512]{1,0:T(8,128)} copy(f32[32,512]{1,0:T(8,128)} %get-tuple-element.4) | data formatting | bytes 131072
  89.4 1.5 %copy.10 = f32[32,512]{1,0:T(8,128)} copy(f32[32,512]{1,0:T(8,128)} %get-tuple-element.5) | data formatting | bytes 131072

commit v3 on v0

v3 whole, which is shorter than its diff:
```python
import jax
import jax.numpy as jnp
from jax import lax
from jax.experimental import pallas as pl
from jax.experimental.pallas import tpu as pltpu
from jax.sharding import PartitionSpec as P

HEAD = 128
EPS = 1e-06
MESH = pl.DeviceIdType.MESH
F32 = jnp.float32
BF16 = jnp.bfloat16
TOKENS = 131072
ROWS = 1024
N_REMOTE = 56 + 4 + 4 * (6 + 3 + 3 + 4) + 1


class Place:
    def __init__(self):
        dp, fs = lax.axis_index("dp"), lax.axis_index("fsdp")
        self.c = dp % 2
        x, z = fs // 8, (fs // 2) % 4
        self.at = {
            "a": x + self.c * (z - x),
            "b": z + self.c * (x - z),
            "y": (dp // 2) * 2 + fs % 2,
        }
        self.fs = fs
        self.y_hi = dp // 2
        self.y_lo = fs % 2

        self.sa, self.sb = 8 - 6 * self.c, 2 + 6 * self.c

    def xz(self, a, b):
        return a + self.c * (b - a), b + self.c * (a - b)

    def device(self, axis, step, other=False):
        at = dict(self.at)
        at[axis] = (at[axis] + step) % 4
        x, z = self.xz(at["a"], at["b"])
        core = 1 - self.c if other else self.c
        return ((at["y"] // 2) * 2 + core, x * 8 + z * 2 + at["y"] % 2)

    def sibling(self):
        return (self.y_hi * 2 + 1 - self.c, self.fs)

    def shard(self, a, b, y_lo):
        return a * self.sa + b * self.sb + y_lo

    def block(self, a, b, y, core):
        return a * self.sa + b * self.sb + ((y // 2) * 64 + y % 2) + core * 32


GROUP = 32
MIDDLE = 15500 / 128
SHIFT = 121.0


def encode(x, ref):
    groups = x.shape[0] // GROUP
    x = x.reshape(groups, GROUP, HEAD)
    top = jnp.maximum(jnp.max(jnp.abs(x), axis=1) * 1.01, 1e-30).astype(BF16)
    steps = MIDDLE / top.astype(F32)
    u = x * steps[:, None, :] + MIDDLE
    k = jnp.floor(u)
    code = (jnp.exp2(k - SHIFT) * (1.0 + (u - k))).astype(BF16)
    ref[0:groups * GROUP, :] = code.reshape(groups * GROUP, HEAD)
    if groups < 16:
        top = jnp.concatenate([top.astype(F32), jnp.zeros((16 - groups, HEAD), F32)], axis=0).astype(BF16)
    ref[groups * GROUP:groups * GROUP + 16, :] = top


def decode(ref, rows):
    groups = rows // GROUP
    y = ref[0:rows, :].astype(F32).reshape(groups, GROUP, HEAD)
    top = ref[rows:rows + 16, :].astype(F32)[0:groups] * (1.0 / MIDDLE)
    k = jnp.floor(jnp.log2(y * (1.0 + 1.0 / 512.0)))
    u = (k + (SHIFT - 1.0 - MIDDLE)) + y * jnp.exp2(-k)
    return (u * top[:, None, :]).reshape(rows, HEAD)


def kernel(
    normed, kw, gain, pk, pv, out_k, out_v,
    x, xt, wk, wv, acc, cot, part, o1, r1, o2, r2, r3, r4, probes, landed,
    load_sem, send_sem, recv_sem,
):
    me = Place()
    a, b, yl, c = me.at["a"], me.at["b"], me.y_lo, me.c
    every = range(4)
    count = [0]
    started = []
    sent = []

    def send(src, dst, device, now=True):
        k = count[0]
        count[0] += 1
        copy = pltpu.make_async_remote_copy(
            src_ref=src, dst_ref=dst, send_sem=send_sem.at[k], recv_sem=recv_sem.at[k],
            device_id=device, device_id_type=MESH,
        )
        started.append(copy)
        if now:
            copy.start()
        return copy

    def same(ref, device):
        return send(ref, ref, device)

    def arrive(*copies):
        for copy in copies:
            copy.wait_recv()

    loads = [
        pltpu.make_async_copy(normed.at[pl.ds(i * 256, 256)], x.at[0, pl.ds(i * 256, 256)], load_sem.at[i])
        for i in range(4)
    ]
    for copy in loads:
        copy.start()

    barrier = pltpu.get_barrier_semaphore()
    greeted = [me.device(axis, d) for axis in ("a", "b", "y") for d in (1, 2, 3)]
    greeted += [me.device(axis, d, True) for axis in ("a", "b", "y") for d in (1, 2, 3)]
    greeted.append(me.sibling())
    for device in greeted:
        pl.semaphore_signal(barrier, inc=1, device_id=device, device_id_type=MESH)

    to = {(axis, d): me.device(axis, d) for axis in ("a", "b", "y") for d in (1, 2, 3)}
    AP, AM, BP, BM, YP, YM = (to[k] for k in (("a", 1), ("a", 3), ("b", 1), ("b", 3), ("y", 1), ("y", 3)))
    am, ap, bm, bp = (a + 3) % 4, (a + 1) % 4, (b + 3) % 4, (b + 1) % 4
    ao, bo, yo = (a + 2) % 4, (b + 2) % 4, 1 - yl
    sibling = me.sibling()

    class Gather:
        def __init__(self, w):
            self.w = w
            self.h0, self.h1 = pl.ds(0, HEAD // 2), pl.ds(HEAD // 2, HEAD // 2)

        def over_y(self, at):
            w = self.w
            return same(w.at[0, :, at, yl, self.h0], YP), same(w.at[0, :, at, yl, self.h1], YM)

        def start(self):
            w = self.w
            self.c0 = [same(w.at[0, a, b, yl], to["a", d]) for d in (2, 1, 3)]
            self.d0 = [same(w.at[1, a, b, yl], to["b", d]) for d in (2, 1, 3)]

        def c1(self):
            arrive(*self.c0)
            self.c = same(self.w.at[0, :, b, yl], BP), same(self.w.at[0, :, b, yl], BM)

        def y0(self):
            self.near = self.over_y(b)

        def e0(self):
            arrive(*self.d0)
            w = self.w
            self.e = same(w.at[1, a, :, yl, self.h0], YP), same(w.at[1, a, :, yl, self.h1], YM)

        def s0(self):
            self.s = same(self.w.at[1, a, :, yl], AP), same(self.w.at[1, a, :, yl], AM)

        def s1(self):
            arrive(*self.e)
            self.r = same(self.w.at[1, a, :, yo], AP), same(self.w.at[1, a, :, yo], AM)

        def f1(self):
            w = self.w
            arrive(*self.c)
            self.f = same(w.at[0, :, bm, yl, self.h0], BP), same(w.at[0, :, bp, yl, self.h1], BM)

        def y1(self):
            self.beside = self.over_y(bm) + self.over_y(bp)

        def t0(self):
            w = self.w
            arrive(*self.s)
            self.t = same(w.at[1, am, :, yl, self.h0], AP), same(w.at[1, ap, :, yl, self.h1], AM)

        def t1(self):
            w = self.w
            arrive(*self.r)
            self.u = same(w.at[1, am, :, yo, self.h0], AP), same(w.at[1, ap, :, yo, self.h1], AM)

        def y2(self):
            arrive(*self.f)
            self.far = self.over_y(bo)

    keys, values = Gather(wk), Gather(wv)

    for h in range(2):
        cols = pl.ds(pl.multiple_of(c * 256 + h * HEAD, HEAD), HEAD)
        wk[h, a, b, yl, :, 0:HEAD] = kw[:, cols]
        wk[h, a, b, yl, :, HEAD:2 * HEAD] = pk[:, cols]
        wv[h, a, b, yl] = pv[:, cols]
    pl.semaphore_wait(barrier, len(greeted))
    pair = [send(normed.at[pl.ds(i * 256, 256)], x.at[1, pl.ds(i * 256, 256)], sibling) for i in range(4)]
    values.start()
    keys.start()
    for copy in loads:
        copy.wait()

    def turn(half, blocks):
        for k in blocks:
            xt[half, 4 * k:4 * k + 4] = x[half, :, k * HEAD:(k + 1) * HEAD].T.reshape(4, 32, ROWS)

    def piece(h, halves, shards, first=False, turned=()):
        def add(half):
            lhs = jnp.concatenate(
                [x[half, :, pl.ds(pl.multiple_of(me.shard(i, j, k) * HEAD, HEAD), HEAD)] for i, j, k in shards], axis=1
            )
            rhs = jnp.concatenate([wk[h, i, j, k] for i, j, k in shards], axis=0)
            new = jnp.dot(lhs, rhs, preferred_element_type=F32)
            for k in range(2):
                some = new[:, k * HEAD:(k + 1) * HEAD].reshape(16, 64, HEAD)
                if first:
                    acc[h, half, k] = some
                else:
                    acc[h, half, k] += some

        if len(halves) == 1:
            turn(halves[0], turned)
            add(halves[0])
        else:
            pl.loop(0, 2)(add)

    def cot_k():
        @pl.loop(0, 8)
        def _(n):
            half, at = n // 4, pl.ds((n % 4) * 4, 4)
            g = gain[...]
            for h in range(2):
                alpha = acc[h, half, 0, at].reshape(256, HEAD)
                delta = acc[h, half, 1, at].reshape(256, HEAD)
                inv = lax.rsqrt(jnp.mean(alpha * alpha, axis=1, keepdims=True) + EPS)
                cubed = inv * inv * inv
                along = jnp.sum(alpha * delta, axis=1, keepdims=True) / HEAD
                gt = g * (g * (delta * inv - alpha * (along * cubed)))
                back = gt * inv - alpha * ((jnp.sum(alpha * gt, axis=1, keepdims=True) / HEAD) * cubed)
                cot[pl.ds(pl.multiple_of(n * 256, 256), 256), (2 + h) * HEAD:(3 + h) * HEAD] = back.astype(BF16)

    def cot_v(half):
        @pl.loop(0, 2)
        def _(n):
            at = pl.ds(pl.multiple_of(n * 512, 512), 512)
            rhs = jnp.concatenate(
                [
                    jnp.concatenate([wv[h, i, j, k] for s in range(16) for i, j in (me.xz(s // 4, s % 4),) for k in range(2)], axis=0)
                    for h in range(2)
                ],
                axis=1,
            )
            new = jnp.dot(x[half, at, :], rhs, preferred_element_type=F32)
            cot[pl.ds(pl.multiple_of(half * ROWS + n * 512, 512), 512), 0:2 * HEAD] = new.astype(BF16)

    axes = (("a", "y", "b"), ("a", "b", "y"), ("a", "y", "b"), ("a", "b", "y"))
    first = [{} for _ in axes]

    plan = ((2, 0, 1), (2, 1, 3), (1, 1, 1), (3, 0, 3), (1, 0, 1), (3, 1, 3))

    def kept(q):
        return part.at[q] if q < 2 else acc.at[q - 2, 0]

    def product(q1, step):
        i1 = (me.at["a"] + step) % 4
        blocks = [me.block(i1, k, j, core) for j in every for k in every for core in range(2)]
        lhs = jnp.concatenate([jnp.concatenate([xt[half, k] for k in blocks], axis=0) for half in range(2)], axis=1)
        new = jnp.dot(lhs, cot[:, q1 * HEAD:(q1 + 2) * HEAD], preferred_element_type=F32)
        one = new[:, 0:HEAD]
        two = new[:, HEAD:2 * HEAD].reshape(4, 4, 64, HEAD)
        two = jnp.concatenate([two[j, k] for k in every for j in every], axis=0)
        for q, rows in ((q1, one), (q1 + 1, two)):
            if step == 0:
                kept(q)[0] = rows.reshape(16, 64, HEAD)
                continue
            for slot, (chunk, half, way) in enumerate(plan):
                if chunk != step:
                    continue
                some = rows[half * 512:(half + 1) * 512]
                if slot < 4:
                    ship(q, slot, some)
                else:
                    kept(q)[1, 8 * slot - 32:8 * slot - 24] = some.reshape(8, 64, HEAD)

    def ship(q, slot, rows):
        encode(rows, o1.at[q, slot % 4])
        first[q][slot] = send(o1.at[q, slot % 4], r1.at[q, slot], to["a", plan[slot][2]])

    def relay(q):
        for slot in (4, 5):
            first[q][slot - 4].wait_recv()
            first[q][slot - 4].wait_send()
            sent.append(first[q][slot - 4])
            own = kept(q)[1, 8 * slot - 32:8 * slot - 24].reshape(512, HEAD)
            ship(q, slot, own + decode(r1.at[q, slot - 4], 512))

    s = [None] * 4
    t = [None] * 4
    final = [None] * 4

    def second(q):
        for half, slots in ((0, (3, 4)), (1, (2, 5))):
            at = slice(8 * half, 8 * half + 8)
            total = kept(q)[0, at].reshape(512, HEAD)
            for slot in slots:
                first[q][slot].wait_recv()
                total = total + decode(r1.at[q, slot], 512)
            kept(q)[0, at] = total.reshape(8, 64, HEAD)
        j = me.at[axes[q][1]]
        s[q] = []
        for d in (2, 1, 3):
            encode(kept(q)[0, pl.ds(((j + d) % 4) * 4, 4)].reshape(256, HEAD), o2.at[q, d - 1])
            s[q].append(send(o2.at[q, d - 1], r2.at[q, d - 1], to[axes[q][1], d]))

    def third(q):
        j, k = me.at[axes[q][1]], me.at[axes[q][2]]
        at = pl.ds(j * 4, 4)
        total = kept(q)[0, at].reshape(256, HEAD)
        for n, d in enumerate((2, 1, 3)):
            s[q][n].wait_recv()
            total = total + decode(r2.at[q, d - 1], 256)
        kept(q)[0, at] = total.reshape(4, 64, HEAD)
        axis = axes[q][2]
        rows, others = pl.ds(pl.multiple_of(c * 32, 32), 32), pl.ds(pl.multiple_of((1 - c) * 32, 32), 32)
        t[q] = [send(kept(q).at[0, j * 4 + (k + d) % 4, rows], r3.at[q, d - 1], to[axis, d]) for d in (2, 1, 3)]
        final[q] = [
            send(kept(q).at[0, j * 4 + (k + d) % 4, others], r4.at[q, d - 1], me.device(axis, d, True)) for d in (2, 1, 3)
        ]
        final[q].append(send(kept(q).at[0, j * 4 + k, others], r4.at[q, 3], sibling))

    def last(q):
        arrive(*t[q])
        rows = pl.ds(pl.multiple_of(c * 32, 32), 32)
        total = kept(q)[0, me.at[axes[q][1]] * 4 + me.at[axes[q][2]], rows] + r3[q, 0] + r3[q, 1] + r3[q, 2]
        put(q, c, total * probes[c, q])

    def put(q, core, total):
        out = out_v if q < 2 else out_k
        out[:, pl.ds(pl.multiple_of(core * 256 + (q % 2) * HEAD, HEAD), HEAD)] = total * (1.0 / TOKENS)

    def rows_of_probes():
        for core in range(2):
            n = (me.y_hi * 2 + core) * 8 + me.fs // 4
            i, j = me.xz(n // 8, (n // 2) % 4)
            row = pl.ds(pl.multiple_of((me.fs % 4) * 32, 32), 32)
            for q in range(4):
                rows = wv[q, i, j, n % 2, row, :] if q < 2 else wk[q - 2, i, j, n % 2, row, HEAD:2 * HEAD]
                probes[core, q] = rows.astype(F32)

    values.c1()
    values.y0()
    values.e0()
    values.s0()
    keys.c1()
    keys.y0()
    values.s1()
    keys.e0()
    piece(0, (0,), [(i, b, yl) for i in every], first=True, turned=range(0, 4))
    values.f1()
    keys.s0()
    piece(1, (0,), [(a, j, yl) for j in every], first=True, turned=range(4, 8))
    arrive(*keys.near)
    piece(0, (0,), [(i, b, yo) for i in every], turned=range(12, 16))
    values.y1()
    arrive(*pair)
    values.y2()
    values.t0()
    keys.f1()
    piece(0, (0,), [(i, j, yl) for i in every for j in (bm, bp)], turned=range(24, 32))
    values.t1()
    piece(0, (1,), [(i, b, k) for i in every for k in (yl, yo)]
          + [(i, j, yl) for i in every for j in (bm, bp)], first=True, turned=range(16, 32))
    keys.y1()
    keys.s1()
    piece(1, (0,), [(a, j, yo) for j in every], turned=range(8, 12))
    keys.t0()
    piece(1, (0,), [(i, j, yl) for i in (am, ap) for j in every], turned=range(16, 24))
    piece(1, (1,), [(a, j, k) for j in every for k in (yl, yo)]
          + [(i, j, yl) for i in (am, ap) for j in every], first=True, turned=range(0, 16))
    arrive(*values.near, *values.beside, *values.far, *values.t, *values.u)
    cot_v(0)
    cot_v(1)
    keys.t1()
    piece(1, (0, 1), [(i, j, yo) for i in (am, ap) for j in every])
    arrive(*keys.beside)
    piece(0, (0, 1), [(i, j, yo) for i in every for j in (bm, bp)])
    keys.y2()
    product(0, 2)
    product(0, 1)
    product(0, 3)
    arrive(*keys.t, *keys.u)
    piece(1, (0, 1), [(ao, j, k) for j in every for k in (yl, yo)])
    arrive(*keys.far)
    piece(0, (0, 1), [(i, bo, k) for i in every for k in (yl, yo)])
    rows_of_probes()
    shared = send(probes.at[1 - c], landed, sibling)
    cot_k()
    relay(0)
    product(2, 2)
    product(2, 1)
    product(2, 3)
    product(0, 0)
    relay(1)
    second(0)
    relay(3)
    product(2, 0)
    relay(2)
    second(1)
    second(3)
    second(2)
    third(3)
    third(1)
    third(0)
    third(2)
    last(0)
    last(3)
    last(1)
    last(2)
    arrive(shared)
    for q in (0, 1, 2, 3):
        arrive(*final[q])
        put(q, 1 - c, (r4[q, 0] + r4[q, 1] + r4[q, 2] + r4[q, 3]) * landed[q])
    for copy in started:
        if not any(copy is other for other in sent):
            copy.wait_send()
    assert count[0] == N_REMOTE


def hand_over(k_ref, v_ref, out_k, out_v):
    out_k[...] = k_ref[...]
    out_v[...] = v_ref[...]


def shards(normed, k_weight, k_gain, probe_k, probe_v):
    vmem = pl.BlockSpec(memory_space=pltpu.VMEM)
    out = jax.ShapeDtypeStruct((32, 512), F32)
    diag_k, diag_v = pl.pallas_call(
        kernel,
        name="curvature",
        out_shape=(out, out),
        in_specs=[pl.BlockSpec(memory_space=pl.ANY)] + [vmem] * 4,
        out_specs=(vmem, vmem),
        scratch_shapes=[
            pltpu.VMEM((2, ROWS, 32 * HEAD), BF16),
            pltpu.VMEM((2, 128, 32, ROWS), BF16),
            pltpu.VMEM((2, 4, 4, 2, HEAD, 2 * HEAD), BF16),
            pltpu.VMEM((2, 4, 4, 2, HEAD, HEAD), BF16),
            pltpu.VMEM((2, 2, 2, 16, 64, HEAD), F32),
            pltpu.VMEM((2 * ROWS, 4 * HEAD), BF16),
            pltpu.VMEM((2, 2, 16, 64, HEAD), F32),
            pltpu.VMEM((4, 4, 528, HEAD), BF16),
            pltpu.VMEM((4, 6, 528, HEAD), BF16),
            pltpu.VMEM((4, 3, 272, HEAD), BF16),
            pltpu.VMEM((4, 3, 272, HEAD), BF16),
            pltpu.VMEM((4, 3, 32, HEAD), F32),
            pltpu.VMEM((4, 4, 32, HEAD), F32),
            pltpu.VMEM((2, 4, 32, HEAD), F32),
            pltpu.VMEM((4, 32, HEAD), F32),
            pltpu.SemaphoreType.DMA((4,)),
            pltpu.SemaphoreType.DMA((N_REMOTE,)),
            pltpu.SemaphoreType.DMA((N_REMOTE,)),
        ],
        compiler_params=pltpu.CompilerParams(
            collective_id=0, has_side_effects=True, vmem_limit_bytes=63 * 2**20
        ),
        cost_estimate=pl.CostEstimate(flops=21 * 10**9, bytes_accessed=10**7, transcendentals=0),
    )(normed, k_weight, k_gain.reshape(1, HEAD), probe_k, probe_v)
    return pl.pallas_call(
        hand_over,
        name="hand_over",
        out_shape=(out, out),
        in_specs=[vmem, vmem],
        out_specs=(vmem, vmem),
    )(diag_k, diag_v)


def solution(mesh):
    return jax.shard_map(
        shards,
        mesh=mesh,
        in_specs=(P(("dp", "fsdp"), None), P("fsdp", None), P(), P("fsdp", None), P("fsdp", None)),
        out_specs=(P(("dp", "fsdp"), None), P(("dp", "fsdp"), None)),
        check_vma=False,
    )
```

time: 1290 us -> 88.2 us (0.07)
  waiting for transfers between devices: 1190 us -> 0 us
  Pallas kernels: 0 us -> 87.3 us
  matrix products: 40.2 us -> 0 us
  local copies, waits for them, and re-layouts: 37.2 us -> 0 us
  between operations: 13.9 us -> 0.64 us
    unnamed x6 -> x0, waiting for transfers between devices: 745 us -> none
    all_gather x3 -> x0, waiting for transfers between devices: 416 us -> none  [the longest x1 146 us: shards(): lax.all_gather(probe_v, 'fsdp', axis=0, tiled=True)]
    pallas_call x0 -> x2, Pallas kernels: none -> 87.3 us  [the longest x1 85.8 us: shards(): pl.pallas_call(kernel, name='curvature', out_shape=(out, out), in_specs=[...]
    dot_general x3 -> x0, matrix products: 40.2 us -> none  [the longest x1 17.5 us: shards(): lax.dot_general(normed, cot, (((0,), (0,)), ((), ())), preferred_element_...]
    reduce_scatter x1 -> x0, waiting for transfers between devices: 30.9 us -> none  [shards(): reduced = lax.psum_scatter(reduced, 'dp', scatter_dimension=0, tiled=True)]
    mul x2 -> x0, local copies, waits for them, and re-layouts: 18.1 us -> none  [the longest x1 17.4 us: shards(): term = term * probes.astype(jnp.float32)]
    unnamed x13 -> x0, local copies, waits for them, and re-layouts: 13.6 us -> none
  transfers between devices with their start and end apart: 5 -> 0, of which waited for: 5 -> 0; matrix products, arithmetic and copies ran while one was open for 2% -> 0% of each run, Pallas kernels for 0% -> 0%
where the time goes in v3:
time: 88.2 us; the launch traced here: 88 us
  Pallas kernels  87.3 us (99%)
    pallas_call x1, Pallas kernels, shards(): pl.pallas_call(kernel, name='curvature', out_shape=(out, out), in_specs=[...  85.8 us

profile of v3, /device:TPU:1, one launch (start us, length us, event | category | flops | bytes accessed | tf_op | source)
XLA Modules:
  0.0 88.0 jit_solution(16563232860095474711)
XLA Ops:
  0.6 85.8 %curvature.1 = (f32[32,512]{1,0:T(8,128)}, f32[32,512]{1,0:T(8,128)}) custom-call(bf16[1024,4096]{1,0:T(8,128)(2,1)} %normed.1, bf16[128,512]{1,0:T(8,128)(2,1)} %kw.1, f32[1,128]{1,0:T(1,128)} %bitcast.1, bf16[128,512]{1,0:T(8,128)(2,1)} %pk.1, bf16[128,512]{1,0:T(8,128)(2,1)} %pv.1), custom_call_target="tpu_custom_call" | custom-call | flops 20999999488 | bytes 10000000 | tf_op jit(solution)/shard_map/curvature/pallas_call | solution.py:436
  86.5 1.5 %hand_over.1 = (f32[32,512]{1,0:T(8,128)}, f32[32,512]{1,0:T(8,128)}) custom-call(f32[32,512]{1,0:T(8,128)} %get-tuple-element.4.k_ref, f32[32,512]{1,0:T(8,128)} %get-tuple-element.5.v_ref), custom_call_target="tpu_custom_call" | custom-call | tf_op jit(solution)/shard_map/hand_over/pallas_call | solution.py:467
